TPU v7x, 32 devices: a whole 2x2x4 slice. The times are simulated.
32 devices in a mesh: expert: 8 (over y, x, core), dp: 4 (over z).
Axes of the slice: x: 2, y: 2, z: 4, core: 2. Of those that a mesh axis runs over, the one named last changes fastest.
Arguments:
- tokens: bfloat16 [1024, 4096], P('expert', 'dp'), may hold values from -6 to 6
- cotangent: bfloat16 [1024, 4096], P('expert', 'dp'), may hold values from -6 to 6
- gate_probs: bfloat16 [1024, 8], P('expert'), may hold values from 0.019897461 to 0.3984375
- expert_ids: int32 [1024, 8], P('expert'), may hold values from 0 to 31, all different within a row; in each aligned block of 128 rows (0 to 127, 128 to 255, ...) at most 36 rows name the same one
- gate_weight: bfloat16 [32, 4096, 1024], P('expert', 'dp'), may hold values from -0.09375 to 0.09375
- up_weight: bfloat16 [32, 4096, 1024], P('expert', 'dp'), may hold values from -0.09375 to 0.09375
- down_weight: bfloat16 [32, 1024, 4096], P('expert', None, 'dp'), may hold values from -0.1875 to 0.1875
Outputs:
- grad_tokens: bfloat16 [1024, 4096], P('expert', 'dp')
- grad_gates: float32 [1024, 8], P('expert')
- grad_gate_weight: float32 [32, 4096, 1024], P('expert', 'dp')
- grad_up_weight: float32 [32, 4096, 1024], P('expert', 'dp')
- grad_down_weight: float32 [32, 1024, 4096], P('expert', None, 'dp')
Inputs may be any that keep to these rules, and one draw needn't show every extreme that they name: `expert_ids`: each row names 8 different experts. Among the 128 rows of one group no expert is named more than 36 times, and in every draw some expert is named exactly 36 times by the rows of some group.
All inputs are finite; a program needn't handle non-finite values.
Results may differ from a plain program's by a relative error of at most 0.012.
Values may be sent and summed in bfloat16 or wider, within the bound.
No kernel may reach another device: no remote copies, remote signals or barrier semaphores. Data moves between devices by JAX's collectives and lax.ppermute only.
A program may use at most 192 MiB of HBM per device.

v0:
```python
import jax
import jax.numpy as jnp
from jax import lax
from jax.sharding import PartitionSpec as P

TOP = 8
EXPERTS = 32
CAP = 36


def local_slots(expert_ids):
    flat_ids = expert_ids.reshape(-1)
    columns = jnp.arange(EXPERTS, dtype=jnp.int32)
    member = (flat_ids[:, None] == columns[None, :]).astype(jnp.int32)
    ranked = jnp.cumsum(member, axis=0) - 1
    within = jnp.sum(member * ranked, axis=1)
    return flat_ids * CAP + within


def pack_rows(tokens, cotangent, gate_probs, target):
    token_count = tokens.shape[0]
    slot_total = EXPERTS * CAP
    slot_index = jnp.arange(slot_total, dtype=jnp.int32)
    placed = target[None, :] == slot_index[:, None]
    chosen = jnp.any(placed.reshape(slot_total, token_count, TOP), axis=2).astype(jnp.bfloat16)
    x_send = jnp.dot(chosen, tokens, preferred_element_type=jnp.float32).astype(jnp.bfloat16)
    dy_send = jnp.dot(chosen, cotangent, preferred_element_type=jnp.float32).astype(jnp.bfloat16)
    weights_flat = gate_probs.reshape(-1).astype(jnp.float32)
    g_send = jnp.sum(jnp.where(placed, weights_flat[None, :], 0.0), axis=1).astype(jnp.bfloat16)
    return (x_send, dy_send, g_send)


def hidden_units(gate_pre, up_pre, back_hidden, g_rows):
    sigmoid_gate = jax.nn.sigmoid(gate_pre)
    swish_gate = gate_pre * sigmoid_gate
    hidden = (swish_gate * up_pre).astype(jnp.bfloat16)
    product = back_hidden * hidden.astype(jnp.float32)
    grad_hidden = g_rows * back_hidden
    derivative = sigmoid_gate * (1.0 + gate_pre * (1.0 - sigmoid_gate))
    grad_gate_pre = (grad_hidden * up_pre * derivative).astype(jnp.bfloat16)
    grad_up_pre = (grad_hidden * swish_gate).astype(jnp.bfloat16)
    return (hidden, grad_gate_pre, grad_up_pre, product)


def shards(tokens, cotangent, gate_probs, expert_ids, gate_weight, up_weight, down_weight):
    expert_count = lax.axis_size("expert")
    data_count = lax.axis_size("dp")
    local_count = gate_weight.shape[0]
    width_part = tokens.shape[1]
    token_count = tokens.shape[0]
    target = local_slots(expert_ids)
    x_send, dy_send, g_send = pack_rows(tokens, cotangent, gate_probs, target)
    x_recv, dy_recv, g_recv = (
        lax.all_to_all(x_send, "expert", split_axis=0, concat_axis=0, tiled=True),
        lax.all_to_all(dy_send, "expert", split_axis=0, concat_axis=0, tiled=True),
        lax.all_to_all(g_send, "expert", split_axis=0, concat_axis=0, tiled=True),
    )
    x_grid = x_recv.reshape(expert_count, local_count, CAP, width_part)
    dy_grid = dy_recv.reshape(expert_count, local_count, CAP, width_part)
    g_grid = g_recv.reshape(expert_count, local_count, CAP)
    g_rows = jnp.transpose(g_grid, (1, 0, 2)).astype(jnp.float32)[..., None]
    gate_part = jnp.einsum(
        "secd,edf->escf", x_grid, gate_weight, preferred_element_type=jnp.float32
    )
    up_part = jnp.einsum("secd,edf->escf", x_grid, up_weight, preferred_element_type=jnp.float32)
    back_part = jnp.einsum(
        "secd,efd->escf", dy_grid, down_weight, preferred_element_type=jnp.float32
    )
    gate_pre, up_pre, back_hidden = (
        lax.psum_scatter(gate_part, "dp", scatter_dimension=3, tiled=True),
        lax.psum_scatter(up_part, "dp", scatter_dimension=3, tiled=True),
        lax.psum_scatter(back_part, "dp", scatter_dimension=3, tiled=True),
    )
    hidden, grad_gate_pre, grad_up_pre, product = hidden_units(
        gate_pre, up_pre, back_hidden, g_rows
    )
    block_sum = jnp.sum(product, axis=3, keepdims=True).astype(jnp.bfloat16)
    hidden_all, gate_grad_all, up_grad_all, gate_blocks = (
        lax.all_gather(hidden, "dp", axis=3, tiled=True),
        lax.all_gather(grad_gate_pre, "dp", axis=3, tiled=True),
        lax.all_gather(grad_up_pre, "dp", axis=3, tiled=True),
        lax.all_gather(block_sum, "dp", axis=3, tiled=True),
    )
    input_terms = jnp.einsum(
        "escf,edf->secd", gate_grad_all, gate_weight, preferred_element_type=jnp.float32
    )
    input_terms = input_terms + jnp.einsum(
        "escf,edf->secd", up_grad_all, up_weight, preferred_element_type=jnp.float32
    )
    input_part = input_terms.astype(jnp.bfloat16).reshape(
        expert_count * local_count * CAP, width_part
    )
    scaled_dy = dy_grid * g_grid[..., None]
    grad_down = jnp.einsum(
        "escf,secd->efd", hidden_all, scaled_dy, preferred_element_type=jnp.float32
    )
    grad_gate = jnp.einsum(
        "secd,escf->edf", x_grid, gate_grad_all, preferred_element_type=jnp.float32
    )
    grad_up = jnp.einsum("secd,escf->edf", x_grid, up_grad_all, preferred_element_type=jnp.float32)
    block_send = jnp.transpose(gate_blocks, (1, 0, 2, 3)).reshape(
        expert_count * local_count * CAP, data_count
    )
    input_table, gate_table = (
        lax.all_to_all(input_part, "expert", split_axis=0, concat_axis=0, tiled=True),
        lax.all_to_all(block_send, "expert", split_axis=0, concat_axis=0, tiled=True),
    )
    picked = jnp.take(input_table, target, axis=0).astype(jnp.float32)
    grad_tokens = picked.reshape(token_count, TOP, width_part).sum(1).astype(jnp.bfloat16)
    grad_gates = (
        jnp.take(gate_table, target, axis=0).astype(jnp.float32).sum(1).reshape(token_count, TOP)
    )
    return (grad_tokens, grad_gates, grad_gate, grad_up, grad_down)


def solution(mesh):
    placed = (
        P("expert", "dp"),
        P("expert", "dp"),
        P("expert", None),
        P("expert", None),
        P("expert", "dp", None),
        P("expert", "dp", None),
        P("expert", None, "dp"),
    )
    return jax.shard_map(
        shards,
        mesh=mesh,
        in_specs=placed,
        out_specs=(
            P("expert", "dp"),
            P("expert", None),
            P("expert", "dp", None),
            P("expert", "dp", None),
            P("expert", None, "dp"),
        ),
        check_vma=False,
    )
```

profile of v0, /device:TPU:0, one launch (start us, length us, event | category | flops | bytes accessed | tf_op | source)
XLA Modules:
  0.0 551.9 jit_solution(1271970343669041624)
XLA Ops:
  8.3 9.0 %reduce-window.6 = s32[32,8,128]{2,1,0:T(8,128)S(1)} reduce-window(s32[32,8,128]{2,1,0:T(8,128)S(1)} %fusion.24, s32[]{:T(128)} %constant.25.clone.1), window={size=1x1x128 pad=0_0x0_0x127_0}, to_apply=%region_0.0 | reduce-window | flops 4161536 | bytes 262148 | tf_op jit(solution)/shard_map/reduce-window
  18.6 4.2 fusion.10
  23.6 34.6 %all_to_all.48 = bf16[8,144,1024]{2,1,0:T(8,128)(2,1)S(1)} all-to-all(bf16[8,144,1024]{2,1,0:T(8,128)(2,1)S(1)} %bitcast.81), channel_id=1, replica_groups=mesh['expert'=8,'dp'=4] {'expert'}, dimensions={0} | all-to-all | bytes 4718592 | tf_op jit(solution)/shard_map/all_to_all | solution.py:55
  58.2 1.3 copy.91
  59.5 5.5 fusion.4
  66.7 31.9 %all_to_all.49 = bf16[8,144,1024]{2,1,0:T(8,128)(2,1)S(1)} all-to-all(bf16[8,144,1024]{2,1,0:T(8,128)(2,1)S(1)} %bitcast.79), channel_id=1, replica_groups=mesh['expert'=8,'dp'=4] {'expert'}, dimensions={0} | all-to-all | bytes 4718592 | tf_op jit(solution)/shard_map/all_to_all | solution.py:54
  99.9 1.5 copy-done.2
  101.4 10.5 %fusion.2 = f32[4,8,36,1024]{3,2,1,0:T(8,128)} fusion(bf16[4,1024,1024]{2,1,0:T(8,128)(2,1)} %param.11, bf16[8,4,36,1024]{3,0,2,1:T(8,128)(2,1)S(1)} %bitcast.82), kind=kOutput, calls=%fused_computation.7 | convolution fusion | flops 2415919104 | bytes 15466496 | tf_op jit(solution)/shard_map/secd,edf->escf/dot_general | solution.py:62
  112.2 10.3 %fusion.8 = f32[4,8,36,1024]{3,2,1,0:T(8,128)} fusion(bf16[4,1024,1024]{2,1,0:T(8,128)(2,1)} %param.12, bf16[8,4,36,1024]{3,0,2,1:T(8,128)(2,1)} %bitcast.83), kind=kOutput, calls=%fused_computation.13 | convolution fusion | flops 2415919104 | bytes 15466496 | tf_op jit(solution)/shard_map/secd,edf->escf/dot_general | solution.py:65
  124.0 7.1 %all_to_all.50 = bf16[8,144,1]{1,2,0:T(2,128)(2,1)S(1)} all-to-all(bf16[8,144,1]{1,2,0:T(2,128)(2,1)S(1)} %convert_element_type.99), channel_id=1, replica_groups=mesh['expert'=8,'dp'=4] {'expert'}, dimensions={0} | all-to-all | bytes 4608 | tf_op jit(solution)/shard_map/all_to_all | solution.py:56
  131.3 27.0 %reduce-scatter.4.cloned.1.call-done = f32[4,8,36,256]{3,2,1,0:T(8,128)} async-done(((f32[4,8,36,1024]{3,2,1,0:T(8,128)}), f32[4,8,36,256]{3,2,1,0:T(8,128)}) %reduce-scatter.4.cloned.1.call-update) | async-done | bytes 1179664 | tf_op jit(solution)/shard_map/reduce_scatter | solution.py:72
  158.3 97.2 %reduce-scatter.8.cloned.1.call-done = f32[4,8,36,256]{3,2,1,0:T(8,128)} async-done(((f32[4,8,36,1024]{3,2,1,0:T(8,128)}), f32[4,8,36,256]{3,2,1,0:T(8,128)}) %reduce-scatter.8.cloned.1.call-update) | async-done | bytes 1179664 | tf_op jit(solution)/shard_map/reduce_scatter | solution.py:70
  255.5 97.2 %reduce-scatter.6.cloned.1.call-done = f32[4,8,36,256]{3,2,1,0:T(8,128)} async-done(((f32[4,8,36,1024]{3,2,1,0:T(8,128)}), f32[4,8,36,256]{3,2,1,0:T(8,128)}) %reduce-scatter.6.cloned.1.call-update) | async-done | bytes 1179664 | tf_op jit(solution)/shard_map/reduce_scatter | solution.py:71
  352.7 4.2 multiply_reduce_fusion
  358.6 13.8 %all_gather.14 = bf16[4,8,36,4]{2,1,0,3:T(8,128)(2,1)S(1)} all-gather(bf16[4,8,36,1]{2,1,0,3:T(8,128)(2,1)S(1)} %bitcast.89), channel_id=1, replica_groups=mesh['expert'=8,'dp'=4] {'dp'}, dimensions={3}, use_global_device_ids=true | all-gather | bytes 11520 | tf_op jit(solution)/shard_map/all_gather | solution.py:82
  373.1 3.6 all-to-all-start.4
  376.8 1.6 broadcast_multiply_fusion
  378.4 3.1 all-to-all-done.4
  381.8 3.2 gather_fusion.1
  386.0 26.4 %all-gather.4.cloned.1.call-done = bf16[4,8,36,1024]{3,2,1,0:T(8,128)(2,1)} async-done(((bf16[4,8,36,256]{3,2,1,0:T(8,128)(2,1)}), bf16[4,8,36,1024]{3,2,1,0:T(8,128)(2,1)}) %all-gather.4.cloned.1.call-update) | async-done | bytes 2359312 | tf_op jit(solution)/shard_map/all_gather | solution.py:80
  412.5 9.5 %fusion = f32[4,8,36,1024]{3,2,1,0:T(8,128)} fusion(bf16[4,8,36,1024]{3,2,1,0:T(8,128)(2,1)} %all-gather.4.cloned.1.call-done, bf16[4,1024,1024]{2,1,0:T(8,128)(2,1)} %param.11), kind=kOutput, calls=%fused_computation.5 | convolution fusion | flops 2415919104 | bytes 15466496 | tf_op jit(solution)/shard_map/escf,edf->secd/dot_general | solution.py:84
  422.0 45.6 %all-gather.6.cloned.1.call-done = bf16[4,8,36,1024]{3,2,1,0:T(8,128)(2,1)} async-done(((bf16[4,8,36,256]{3,2,1,0:T(8,128)(2,1)}), bf16[4,8,36,1024]{3,2,1,0:T(8,128)(2,1)}) %all-gather.6.cloned.1.call-update) | async-done | bytes 2359312 | tf_op jit(solution)/shard_map/all_gather | solution.py:81
  467.6 8.5 %fusion.11 = bf16[8,4,36,1024]{3,2,0,1:T(8,128)(2,1)S(1)} fusion(f32[4,8,36,1024]{3,2,1,0:T(8,128)} %fusion, bf16[4,8,36,1024]{3,2,1,0:T(8,128)(2,1)} %all-gather.6.cloned.1.call-done, bf16[4,1024,1024]{2,1,0:T(8,128)(2,1)} %param.12), kind=kOutput, calls=%fused_computation.22 | convolution fusion | flops 2418278400 | bytes 17825792 | tf_op jit(solution)/shard_map/escf,edf->secd/dot_general | solution.py:87
  476.1 1.3 copy.96
  477.4 2.7 copy.97
  480.2 13.6 %all-to-all-start.3 = ((bf16[8,144,1024]{2,1,0:T(8,128)(2,1)}), bf16[8,144,1024]{2,1,0:T(8,128)(2,1)}, u32[]{:S(2)}, u32[]{:S(2)}) async-start(bf16[8,144,1024]{2,1,0:T(8,128)(2,1)} %copy.97), calls=%async_computation.6 | async-start | bytes 4718592 | tf_op jit(solution)/shard_map/all_to_all | solution.py:105
  493.8 10.8 %convolution_bitcast_fusion = f32[4,1024,1024]{2,1,0:T(8,128)} fusion(bf16[8,4,36,1024]{3,0,2,1:T(8,128)(2,1)S(1)} %bitcast.84, bf16[4,8,36,1024]{3,2,1,0:T(8,128)(2,1)} %all-gather.6.cloned.1.call-done), kind=kOutput, calls=%fused_computation.2 | convolution fusion | flops 2415919104 | bytes 21495808 | tf_op jit(solution)/shard_map/secd,escf->edf/dot_general | solution.py:100
  504.6 8.8 %convolution_bitcast_fusion.1 = f32[4,1024,1024]{2,1,0:T(8,128)} fusion(bf16[8,4,36,1024]{3,0,2,1:T(8,128)(2,1)S(1)} %bitcast.85, bf16[4,8,36,1024]{3,2,1,0:T(8,128)(2,1)S(1)} %copy-done.11), kind=kOutput, calls=%fused_computation.3 | convolution fusion | flops 2415919104 | bytes 21495808 | tf_op jit(solution)/shard_map/secd,escf->edf/dot_general | solution.py:97
  513.3 8.7 %all-gather.8.cloned.1.call-done = bf16[4,8,36,1024]{3,2,1,0:T(8,128)(2,1)} async-done(((bf16[4,8,36,256]{3,2,1,0:T(8,128)(2,1)}), bf16[4,8,36,1024]{3,2,1,0:T(8,128)(2,1)}) %all-gather.8.cloned.1.call-update) | async-done | bytes 2359312 | tf_op jit(solution)/shard_map/all_gather | solution.py:79
  522.1 14.0 %convolution_bitcast_fusion.2 = f32[4,1024,1024]{2,1,0:T(8,128)} fusion(bf16[4,8,36,1024]{3,2,1,0:T(8,128)(2,1)} %all-gather.8.cloned.1.call-done, bf16[8,4,36,1024]{3,0,2,1:T(8,128)(2,1)} %broadcast_multiply_fusion), kind=kOutput, calls=%fused_computation.4 | convolution fusion | flops 2415919104 | bytes 21495808 | tf_op jit(solution)/shard_map/escf,secd->efd/dot_general | solution.py:94
  536.1 7.0 %gather_fusion = bf16[1024,1024]{1,0:T(8,128)(2,1)S(1)} fusion(bf16[1152,1024]{1,0:T(8,128)(2,1)} %bitcast.16, s32[1024]{0:T(1024)S(1)} %copy-done.7), kind=kCustom, calls=%fused_computation | custom fusion | bytes 4198400 | tf_op jit(solution)/shard_map/jit(_take)/gather | solution.py:108
  543.1 1.8 fusion.18
  (75 shorter events, 11.9 us)
Async XLA Ops:
  7.2 15.6 %copy-start = (bf16[128,1024]{1,0:T(8,128)(2,1)S(1)}, bf16[128,1024]{1,0:T(8,128)(2,1)}, u32[]{:S(2)}) copy-start(bf16[128,1024]{1,0:T(8,128)(2,1)} %param.8) | copy-start | bytes 786436
  7.2 151.1 %reduce-scatter.4.cloned.1.call-start = ((), (), s32[]{:S(2)}) async-start(), calls=%async_computation.8 | async-start | bytes 6553600 | tf_op jit(solution)/shard_map/reduce_scatter | solution.py:72
  23.6 35.9 %copy-start.10 = (bf16[4,1024,1024]{2,1,0:T(8,128)(2,1)S(1)}, bf16[4,1024,1024]{2,1,0:T(8,128)(2,1)}, u32[]{:S(2)}) copy-start(bf16[4,1024,1024]{2,1,0:T(8,128)(2,1)} %param.13) | copy-start | bytes 25165828
  65.0 0.9 copy-start.4
  65.0 190.5 %reduce-scatter.8.cloned.1.call-start = ((), (), s32[]{:S(2)}) async-start(), calls=%async_computation.10 | async-start | bytes 6553600 | tf_op jit(solution)/shard_map/reduce_scatter | solution.py:70
  99.9 1.5 copy-start.2
  111.9 240.8 %reduce-scatter.6.cloned.1.call-start = ((), (), s32[]{:S(2)}) async-start(), calls=%async_computation.9 | async-start | bytes 6553600 | tf_op jit(solution)/shard_map/reduce_scatter | solution.py:71
  122.5 0.7 copy-start.9
  122.5 290.0 %all-gather.4.cloned.1.call-start = ((), (), s32[]{:S(2)}) async-start(), calls=%async_computation.11 | async-start | bytes 3276800 | tf_op jit(solution)/shard_map/all_gather | solution.py:80
  131.2 226.2 %copy-start.8 = (s32[128,8]{0,1:T(8,128)S(1)}, s32[128,8]{0,1:T(8,128)}, u32[]{:S(2)}) copy-start(s32[128,8]{0,1:T(8,128)} %param.10) | copy-start | bytes 12292
  356.9 110.7 %all-gather.6.cloned.1.call-start = ((), (), s32[]{:S(2)}) async-start(), calls=%async_computation.12 | async-start | bytes 3276800 | tf_op jit(solution)/shard_map/all_gather | solution.py:81
  358.5 23.3 %copy-start.6 = (s32[1024]{0:T(1024)}, s32[1024]{0:T(1024)S(1)}, u32[]{:S(2)}) copy-start(s32[1024]{0:T(1024)S(1)} %broadcast_clamp_fusion) | copy-start | bytes 12292
  373.1 8.4 %all-to-all-start.4 = ((bf16[8,144,4]{1,2,0:T(4,128)(2,1)}), bf16[8,144,4]{1,2,0:T(4,128)(2,1)S(1)}, u32[]{:S(2)}, u32[]{:S(2)}) async-start(bf16[8,144,4]{1,2,0:T(4,128)(2,1)} %reshape.181), calls=%async_computation.7 | async-start | bytes 32768 | tf_op jit(solution)/shard_map/all_to_all | solution.py:106
  376.7 145.3 %all-gather.8.cloned.1.call-start = ((), (), s32[]{:S(2)}) async-start(), calls=%async_computation.13 | async-start | bytes 3276800 | tf_op jit(solution)/shard_map/all_gather | solution.py:79
  480.2 13.6 %copy-start.3 = (bf16[8,144,1024]{2,0,1:T(8,128)(2,1)S(1)}, bf16[8,144,1024]{2,0,1:T(8,128)(2,1)}, u32[]{:S(2)}) copy-start(bf16[8,144,1024]{2,0,1:T(8,128)(2,1)} %copy-done.2) | copy-start | bytes 7077892
  480.2 55.9 %all-to-all-start.3 = ((bf16[8,144,1024]{2,1,0:T(8,128)(2,1)}), bf16[8,144,1024]{2,1,0:T(8,128)(2,1)}, u32[]{:S(2)}, u32[]{:S(2)}) async-start(bf16[8,144,1024]{2,1,0:T(8,128)(2,1)} %copy.97), calls=%async_computation.6 | async-start | bytes 4718592 | tf_op jit(solution)/shard_map/all_to_all | solution.py:105
  493.7 10.8 %copy-start.11 = (bf16[4,8,36,1024]{3,2,1,0:T(8,128)(2,1)S(1)}, bf16[4,8,36,1024]{3,2,1,0:T(8,128)(2,1)}, u32[]{:S(2)}) copy-start(bf16[4,8,36,1024]{3,2,1,0:T(8,128)(2,1)} %all-gather.4.cloned.1.call-done) | copy-start | bytes 7077892
  513.3 22.7 %copy-start.7 = (s32[1024]{0:T(1024)S(1)}, s32[1024]{0:T(1024)}, u32[]{:S(2)}) copy-start(s32[1024]{0:T(1024)} %copy-done.6) | copy-start | bytes 12292
  536.1 7.0 %copy-start.5 = (pred[128,8]{1,0:T(8,128)(4,1)S(1)}, pred[128,8]{1,0:T(8,128)(4,1)}, u32[]{:S(2)}) copy-start(pred[128,8]{1,0:T(8,128)(4,1)} %copy.87) | copy-start | bytes 3076
  536.1 8.8 %copy-start.1 = (bf16[128,1024]{1,0:T(8,128)(2,1)S(1)}, bf16[128,1024]{1,0:T(8,128)(2,1)}, u32[]{:S(2)}) copy-start(bf16[128,1024]{1,0:T(8,128)(2,1)} %param.8) | copy-start | bytes 786436
Sparse Core Ops, SparseCore 0:
  65.2 93.0 reduce-scatter.3
  161.2 94.2 reduce-scatter.7
  258.4 94.2 reduce-scatter.5
  357.0 55.4 all-gather.3
  414.5 53.0 all-gather.5
  469.0 53.0 all-gather.7
where the time goes:
time: 561 us; the launch traced here: 552 us
  waiting for transfers between devices  306 us (55%)
  blocking collectives  87.4 us (16%)
  matrix products  79.4 us (14%)
  local copies, waits for them, and re-layouts  24.4 us (4%)
  other arithmetic  22.6 us (4%)
  starting transfers between devices  17.7 us (3%)
  between operations  14.6 us (3%)
    reduce_scatter x1, waiting for transfers between devices, shards(): lax.psum_scatter(gate_part, 'dp', scatter_dimension=3, tiled=True)  97.2 us
    reduce_scatter x1, waiting for transfers between devices, shards(): lax.psum_scatter(up_part, 'dp', scatter_dimension=3, tiled=True)  97.2 us
    all_gather x1, waiting for transfers between devices, shards(): lax.all_gather(grad_up_pre, 'dp', axis=3, tiled=True)  45.6 us
    all_to_all x1, blocking collectives, shards(): lax.all_to_all(dy_send, 'expert', split_axis=0, concat_axis=0, tiled=True)  34.6 us
    all_to_all x1, blocking collectives, shards(): lax.all_to_all(x_send, 'expert', split_axis=0, concat_axis=0, tiled=True)  31.9 us
    reduce_scatter x1, waiting for transfers between devices, shards(): lax.psum_scatter(back_part, 'dp', scatter_dimension=3, tiled=True)  27 us
    all_gather x1, waiting for transfers between devices, shards(): lax.all_gather(grad_gate_pre, 'dp', axis=3, tiled=True)  26.4 us
    dot_general x1, matrix products, shards(): jnp.einsum('escf,secd->efd', hidden_all, scaled_dy, preferred_element_typ...  14 us
  transfers between devices with their start and end apart: 8, of which 7 were waited for; matrix products, arithmetic and copies ran while one was open for 16% of the time, Pallas kernels for 0%

commit v1 on v0

v1 whole, which is shorter than its diff:
```python
import functools

import jax
import jax.numpy as jnp
from jax import lax
from jax.experimental import pallas as pl
from jax.experimental.pallas import tpu as pltpu
from jax.sharding import PartitionSpec as P

TOP = 8
EXPERTS = 32
CAP = 36
VMEM_BYTES = 56 * 1024 * 1024
F32 = jnp.float32
BF16 = jnp.bfloat16
ANY = pl.BlockSpec(memory_space=pl.ANY)


def params():
    return pltpu.CompilerParams(vmem_limit_bytes=VMEM_BYTES)


def nt_dot(a, b):
    return lax.dot_general(a, b, (((1,), (1,)), ((), ())), preferred_element_type=F32)


def forward_body(blocks, me_ref, x_ref, dy_ref, gate_ref, up_ref, down_ref, *rest):
    out_ref, first_ref = rest[-2:]
    step = pl.program_id(1)
    out_ref[0, 0] = jnp.dot(x_ref[...], gate_ref[0], preferred_element_type=F32).astype(BF16)
    out_ref[0, 1] = jnp.dot(x_ref[...], up_ref[0], preferred_element_type=F32).astype(BF16)
    out_ref[0, 2] = nt_dot(dy_ref[...], down_ref[0]).astype(BF16)
    wanted = jnp.where(me_ref[0] == 0, blocks - 1, 1)

    @pl.when(step == wanted)
    def _():
        first_ref[...] = out_ref[0]


def forward(me, x, dy, gate_w, up_w, down_w, start, count, blocks, deps):
    rows = x.shape[0] // count
    width = x.shape[1]
    fb = gate_w.shape[2] // blocks
    total = x.shape[0]
    flops = 6 * total * width * fb * blocks
    return pl.pallas_call(
        functools.partial(forward_body, blocks),
        out_shape=(
            jax.ShapeDtypeStruct((blocks, 3, total, fb), BF16),
            jax.ShapeDtypeStruct((3, total, fb), BF16),
        ),
        grid_spec=pltpu.PrefetchScalarGridSpec(
            num_scalar_prefetch=1,
            grid=(count, blocks),
            in_specs=[
                pl.BlockSpec((rows, width), lambda i, k, m: (i, 0)),
                pl.BlockSpec((rows, width), lambda i, k, m: (i, 0)),
                pl.BlockSpec((1, width, fb), lambda i, k, m: (start + i, 0, (m[0] + k) % blocks)),
                pl.BlockSpec((1, width, fb), lambda i, k, m: (start + i, 0, (m[0] + k) % blocks)),
                pl.BlockSpec((1, fb, width), lambda i, k, m: (start + i, (m[0] + k) % blocks, 0)),
            ]
            + [ANY] * len(deps),
            out_specs=[
                pl.BlockSpec((1, 3, rows, fb), lambda i, k, m: (k, 0, i, 0)),
                pl.BlockSpec((3, rows, fb), lambda i, k, m: (0, i, 0)),
            ],
        ),
        compiler_params=params(),
        cost_estimate=pl.CostEstimate(
            flops=flops, bytes_accessed=count * 6 * width * fb * blocks, transcendentals=0
        ),
        name="forward_products",
    )(me, x, dy, gate_w, up_w, down_w, *deps)


def add_body(pairs, *refs):
    outs = refs[-pairs:]
    for at in range(pairs):
        own, got = refs[2 * at], refs[2 * at + 1]
        outs[at][...] = (own[0].astype(F32) + got[...].astype(F32)).astype(BF16)


def add_blocks(parts, places, received, deps):
    _, three, rows, fb = parts.shape
    pairs = len(places)
    operands, specs = [], []
    for place, got in zip(places, received):
        operands += [parts, got]
        specs += [
            pl.BlockSpec((1, 1, rows, fb), lambda i, place=place: (place, i, 0, 0)),
            pl.BlockSpec((1, rows, fb), lambda i: (i, 0, 0)),
        ]
    return pl.pallas_call(
        functools.partial(add_body, pairs),
        out_shape=[jax.ShapeDtypeStruct((three, rows, fb), BF16)] * pairs,
        grid=(three,),
        in_specs=specs + [ANY] * len(deps),
        out_specs=[pl.BlockSpec((1, rows, fb), lambda i: (i, 0, 0))] * pairs,
        compiler_params=params(),
        cost_estimate=pl.CostEstimate(
            flops=pairs * three * rows * fb,
            bytes_accessed=pairs * 6 * three * rows * fb,
            transcendentals=0,
        ),
        name="hop_sum",
    )(*operands, *deps)


def join_body(a_ref, b_ref, *rest):
    rest[-1][...] = a_ref[...] + b_ref[...]


def join(a, b, deps):
    return pl.pallas_call(
        join_body,
        out_shape=jax.ShapeDtypeStruct(a.shape, BF16),
        in_specs=[pl.BlockSpec(memory_space=pltpu.VMEM)] * 2 + [ANY] * len(deps),
        out_specs=pl.BlockSpec(memory_space=pltpu.VMEM),
        compiler_params=params(),
        cost_estimate=pl.CostEstimate(
            flops=a.size, bytes_accessed=6 * a.size, transcendentals=0
        ),
        name="hop_join",
    )(a, b, *deps)


def hidden_body(own_ref, right_ref, left_ref, g_ref, *rest):
    out_ref = rest[-1]
    rows = right_ref.shape[1]

    def total(at):
        return (
            own_ref[0, at].astype(F32) + right_ref[at].astype(F32) + left_ref[at].astype(F32)
        )

    gate, up, back = total(0), total(1), total(2)
    sig = jax.nn.sigmoid(gate)
    swish = gate * sig
    hidden = (swish * up).astype(BF16)
    product = back * hidden.astype(F32)
    grad = g_ref[...] * back
    out_ref[0:rows] = hidden
    out_ref[rows : 2 * rows] = (grad * up * (sig * (1.0 + gate * (1.0 - sig)))).astype(BF16)
    out_ref[2 * rows : 3 * rows] = (grad * swish).astype(BF16)
    high = product.astype(BF16)
    low = (product - high.astype(F32)).astype(BF16)
    fb = product.shape[1]
    ones = jnp.ones((16, fb), BF16)
    for part in range(-(-rows // fb)):
        lo, hi = part * fb, min(rows, part * fb + fb)
        sums = nt_dot(ones, high[lo:hi]) + nt_dot(ones, low[lo:hi])
        base = 3 * rows + 16 * part
        if hi - lo < fb:
            out_ref[base : base + 16] = jnp.zeros((16, fb), BF16)
        out_ref[base : base + 16, 0 : hi - lo] = sums.astype(BF16)


def hidden_units(parts, right, left, g_rows, deps):
    three, rows, fb = right.shape
    return pl.pallas_call(
        hidden_body,
        out_shape=jax.ShapeDtypeStruct((3 * rows + 16 * (-(-rows // fb)), fb), BF16),
        grid=(1,),
        in_specs=[
            pl.BlockSpec((1, 3, rows, fb), lambda i: (0, 0, 0, 0)),
            pl.BlockSpec((3, rows, fb), lambda i: (0, 0, 0)),
            pl.BlockSpec((3, rows, fb), lambda i: (0, 0, 0)),
            pl.BlockSpec((rows, 1), lambda i: (0, 0)),
        ]
        + [ANY] * len(deps),
        out_specs=pl.BlockSpec((3 * rows + 16 * (-(-rows // fb)), fb), lambda i: (0, 0)),
        compiler_params=params(),
        cost_estimate=pl.CostEstimate(
            flops=30 * rows * fb, bytes_accessed=24 * rows * fb, transcendentals=rows * fb
        ),
        name="hidden_units",
    )(parts, right, left, g_rows, *deps)


def pass_body(*refs):
    pass


def pass_on(a, b, deps):
    shape = jax.ShapeDtypeStruct(a.shape, a.dtype)
    return pl.pallas_call(
        pass_body,
        out_shape=[shape, shape],
        in_specs=[ANY] * (2 + len(deps)),
        out_specs=[ANY, ANY],
        input_output_aliases={0: 0, 1: 1},
        compiler_params=params(),
        cost_estimate=pl.CostEstimate(flops=0, bytes_accessed=0, transcendentals=0),
        name="hop_forward",
    )(a, b, *deps)


def expert_body(place, near_rows, far_rows, aliased, me_ref, *refs):
    near, far = refs[0:5], refs[5:10]
    near_x, near_dy, far_x, far_dy, gate_ref, up_ref = refs[10:16]
    grad_gate, grad_up, grad_down, rows_ref = refs[-8:-4]
    act, xs, dys, total = refs[-4:]
    step = pl.program_id(0)
    last = pl.num_programs(0) - 1
    me = me_ref[0]
    near_total = near_x.shape[0]
    at = place * near_rows

    def fill(which):
        for j in range(3):
            act[j, 0:near_rows] = near[which][pl.ds(j * near_total + at, near_rows)]
            act[j, near_rows:] = far[which][pl.ds(j * far_rows, far_rows)]

    @pl.when(step == 0)
    def _():
        fill(0)
        xs[0:near_rows] = near_x[pl.ds(at, near_rows)]
        xs[near_rows:] = far_x[...]
        dys[0:near_rows] = near_dy[pl.ds(at, near_rows)]
        dys[near_rows:] = far_dy[...]
        total[...] = jnp.zeros_like(total)

    @pl.when((step == 1) & (me != last))
    def _():
        fill(1)

    @pl.when((step == last) & (me != 0))
    def _():
        fill(2)

    @pl.when(step == 2)
    def _():
        fill(3)

    @pl.when(((step == 1) & (me == last)) | ((step == last) & (me == 0)))
    def _():
        fill(4)

    hidden, gate_grad, up_grad = act[0], act[1], act[2]
    total[...] += nt_dot(gate_grad, gate_ref[0]) + nt_dot(up_grad, up_ref[0])

    @pl.when(step == last)
    def _():
        rows_ref[...] = total[...].astype(BF16)

    over_rows = (((0,), (0,)), ((), ()))
    grad_gate[0] = lax.dot_general(xs[...], gate_grad, over_rows, preferred_element_type=F32)
    grad_up[0] = lax.dot_general(xs[...], up_grad, over_rows, preferred_element_type=F32)
    grad_down[0] = lax.dot_general(hidden, dys[...], over_rows, preferred_element_type=F32)


def expert_grads(me, place, near, far, near_x, near_dy, far_x, far_dy, weights, earlier, deps):
    gate_w, up_w = weights
    experts, width, ff = gate_w.shape
    fb = near[0].shape[1]
    blocks = ff // fb
    near_rows = near_x.shape[0] // experts
    far_rows = far_x.shape[0]
    rows = near_rows + far_rows

    def whole(a):
        return pl.BlockSpec(a.shape, lambda k, m: (0,) * a.ndim, pipeline_mode=pl.Buffered(1))

    wide = pl.BlockSpec((1, width, fb), lambda k, m: (place, 0, (m[0] + k) % blocks))
    tall = pl.BlockSpec((1, fb, width), lambda k, m: (place, (m[0] + k) % blocks, 0))
    held = [*near, *far, near_x, near_dy, far_x, far_dy]
    operands = [me, *held, gate_w, up_w]
    specs = [whole(a) for a in held] + [wide, wide]
    aliases = {}
    if earlier is not None:
        aliases = {len(operands) + j: j for j in range(3)}
        operands += list(earlier)
        specs += [ANY] * 3
    return pl.pallas_call(
        functools.partial(expert_body, place, near_rows, far_rows, earlier is not None),
        out_shape=(
            jax.ShapeDtypeStruct((experts, width, ff), F32),
            jax.ShapeDtypeStruct((experts, width, ff), F32),
            jax.ShapeDtypeStruct((experts, ff, width), F32),
            jax.ShapeDtypeStruct((rows, width), BF16),
        ),
        grid_spec=pltpu.PrefetchScalarGridSpec(
            num_scalar_prefetch=1,
            grid=(blocks,),
            in_specs=specs + [ANY] * len(deps),
            out_specs=[wide, wide, tall, pl.BlockSpec((rows, width), lambda k, m: (0, 0))],
            scratch_shapes=[
                pltpu.VMEM((3, rows, fb), BF16),
                pltpu.VMEM((rows, width), BF16),
                pltpu.VMEM((rows, width), BF16),
                pltpu.VMEM((rows, width), F32),
            ],
        ),
        input_output_aliases=aliases,
        compiler_params=params(),
        cost_estimate=pl.CostEstimate(
            flops=10 * rows * width * ff, bytes_accessed=16 * width * ff, transcendentals=0
        ),
        name="expert_grads",
    )(*operands, *deps)


def swap(array, bit, count):
    return lax.ppermute(array, "expert", [(i, i ^ (1 << bit)) for i in range(count)])


def spread(own, order, count):
    held = own[None]
    for bit in order:
        held = jnp.concatenate([held, swap(held, bit, count)])
    return held


def offsets(order):
    held = [0]
    for bit in order:
        held = held + [at | (1 << bit) for at in held]
    return held


def reordered(array, have, want):
    if have == want:
        return array
    return jnp.stack([array[have.index(at)] for at in want])


def shards(tokens, cotangent, gate_probs, expert_ids, gate_weight, up_weight, down_weight):
    count = lax.axis_size("expert")
    blocks = lax.axis_size("dp")
    me = lax.axis_index("dp").astype(jnp.int32)
    group = lax.axis_index("expert").astype(jnp.int32)
    me_arg = me.reshape(1)
    local = gate_weight.shape[0]
    group_size, width = tokens.shape
    fb = gate_weight.shape[2] // blocks
    bits = count.bit_length() - 1
    pair = 2

    meta_rows = -(-group_size * TOP // width)
    pad_rows = -(-2 * meta_rows // 16) * 16

    def as_rows(a):
        flat = jnp.pad(a.astype(BF16).reshape(-1), (0, meta_rows * width - a.size))
        return flat.reshape(meta_rows, width)

    meta = jnp.concatenate(
        [
            as_rows(expert_ids),
            as_rows(gate_probs),
            jnp.zeros((pad_rows - 2 * meta_rows, width), BF16),
        ]
    )
    own_x = jnp.concatenate([tokens, meta])
    near_x_all = jnp.stack([own_x, swap(own_x, 0, count)])
    near_dy_all = jnp.stack([cotangent, swap(cotangent, 0, count)])
    ahead = list(range(1, bits))
    chips_x = spread(own_x, ahead, count)
    chips_dy = spread(cotangent, ahead[::-1], count)
    even = [at for at in range(0, count, 2)]
    chips_dy = reordered(chips_dy, offsets(ahead[::-1]), even)
    far_x_all = jnp.stack([chips_x[1:], swap(chips_x[1:], 0, count)], axis=1)
    far_dy_all = jnp.stack([chips_dy[1:], swap(chips_dy[1:], 0, count)], axis=1)
    far_x_all = far_x_all.reshape((count - pair,) + own_x.shape)
    far_dy_all = far_dy_all.reshape((count - pair,) + cotangent.shape)

    def meta_of(a, which):
        part = a[:, group_size + which * meta_rows : group_size + (which + 1) * meta_rows]
        part = part.reshape(a.shape[0], -1)[:, : group_size * TOP]
        return part.reshape(a.shape[0], group_size, TOP)

    experts_here = (group * local + jnp.arange(local, dtype=jnp.int32)).astype(F32)
    before = (
        jnp.arange(group_size)[:, None] < jnp.arange(group_size)[None, :]
    ).astype(BF16)

    def members(a):
        named = meta_of(a, 0).astype(F32)[None] == experts_here[:, None, None, None]
        member = jnp.any(named, axis=3)
        prob = jnp.sum(jnp.where(named, meta_of(a, 1).astype(F32)[None], 0.0), axis=3)
        ranks = jnp.einsum(
            "egt,tu->egu", member.astype(BF16), before, preferred_element_type=F32
        ).astype(jnp.int32)
        return member, prob, ranks

    near_rows = pair * CAP // 16 * 16
    spill = pair * CAP - near_rows
    far_rows = -(-(spill + (count - pair) * CAP) // 16) * 16

    near_member, near_prob, near_rank = members(near_x_all)
    held = jnp.sum(near_member[:, :1].astype(jnp.int32), axis=2, keepdims=True)
    near_rank = jnp.concatenate([near_rank[:, :1], near_rank[:, 1:] + held], axis=1)
    near_rank = jnp.where(near_member, near_rank, -1).reshape(local, -1)
    near_prob = near_prob.reshape(local, -1)
    near_tokens = near_x_all[:, :group_size].reshape(-1, width)
    near_cot = near_dy_all.reshape(-1, width)

    def pick(slot, rows):
        return slot[None, :] == jnp.arange(rows, dtype=jnp.int32)[:, None]

    def gather(chosen, prob, x_all, dy_all):
        hot = chosen.astype(BF16)
        x = jnp.dot(hot, x_all, preferred_element_type=F32).astype(BF16)
        dy32 = jnp.dot(hot, dy_all, preferred_element_type=F32)
        g = jnp.sum(jnp.where(chosen, prob, 0.0), axis=1, keepdims=True)
        return x, dy32.astype(BF16), (dy32 * g).astype(BF16), g

    near_chosen = jnp.concatenate([pick(near_rank[e], near_rows) for e in range(local)])
    near_prob_rows = jnp.repeat(near_prob, near_rows, axis=0)
    near = gather(near_chosen, near_prob_rows, near_tokens, near_cot)

    far_member, far_prob, far_rank = members(far_x_all)
    first = spill + CAP * jnp.arange(count - pair, dtype=jnp.int32)[None, :, None]
    far_slot = jnp.where(far_member, far_rank + first, -1).reshape(local, -1)
    all_slot = jnp.concatenate([jnp.maximum(near_rank - near_rows, -1), far_slot], axis=1)
    all_prob = jnp.concatenate([near_prob, far_prob.reshape(local, -1)], axis=1)
    all_tokens = jnp.concatenate([near_tokens, far_x_all[:, :group_size].reshape(-1, width)])
    all_cot = jnp.concatenate([near_cot, far_dy_all.reshape(-1, width)])

    chunks = [near]
    for e in range(local):
        chosen = pick(all_slot[e], far_rows)
        chunks.append(gather(chosen, all_prob[e][None, :], all_tokens, all_cot))

    up1 = [(0, 1), (blocks - 1, blocks - 2)]
    up2, down2 = [(0, 1), (1, 2)], [(3, 2), (2, 1)]
    up, down = [(0, 1), (1, 2), (2, 3)], [(1, 0), (2, 1), (3, 2)]
    on, back = [(1, 2), (2, 3)], [(2, 1), (1, 0)]
    ends = [(2, 3), (1, 0)]

    def move(a, pairs):
        return lax.ppermute(a, "dp", pairs)

    total_chunks = local + 1
    state = [dict() for _ in range(total_chunks)]
    chain = []
    grads = None
    row_terms = []

    for window in range(2 * (total_chunks - 1) + 7):
        events = [(c, window - 2 * c) for c in range(total_chunks)]
        events = [ev for ev in events if 0 <= ev[1] <= 6]
        events.sort(key=lambda ev: (ev[1] == 6, ev[0]))
        for c, hop in events:
            s = state[c]
            if hop == 0:
                x, dy, _, _ = chunks[c]
                start, amount = (0, local) if c == 0 else (c - 1, 1)
                s["parts"], first_send = forward(
                    me_arg, x, dy, gate_weight, up_weight, down_weight, start, amount, blocks,
                    chain,
                )
                chain = [first_send]
                s["in"] = move(first_send, up1)
            elif hop == 1:
                (send,) = add_blocks(s["parts"], (2,), (s["in"],), chain)
                chain = [send]
                s["right"], s["left"] = move(send, up2), move(send, down2)
            elif hop == 2:
                right, left = add_blocks(
                    s["parts"], (1, 3), (s["right"], s["left"]), chain
                )
                chain = [right]
                s["right"], s["left"] = move(right, up), move(left, down)
            elif hop == 3:
                s["own"] = hidden_units(
                    s["parts"], s["right"], s["left"], chunks[c][3], chain
                )
                chain = [s["own"]]
                s["r1"], s["l1"] = move(s["own"], up), move(s["own"], down)
            elif hop == 4:
                s["r1"], s["l1"] = pass_on(s["r1"], s["l1"], chain)
                chain = [s["r1"]]
                s["r2"], s["l2"] = move(s["r1"], on), move(s["l1"], back)
            elif hop == 5:
                s["g2"] = join(s["r2"], s["l2"], chain)
                chain = [s["g2"]]
                s["x3"] = move(s["g2"], ends)
            else:
                s["all"] = [s[name] for name in ("own", "l1", "r1", "g2", "x3")]
                if c == 0:
                    continue
                *grads, rows = expert_grads(
                    me_arg, c - 1, state[0]["all"], s["all"], near[0], near[2],
                    chunks[c][0], chunks[c][2], (gate_weight, up_weight), grads, chain,
                )
                chain = [rows]
                row_terms.append(rows)

    def gate_sums(c):
        rows = chunks[c][0].shape[0]
        own, l1, r1, g2, x3 = [
            a[3 * rows :].reshape(-1, 16, fb)[:, 0].reshape(-1)[:rows].astype(F32)
            for a in state[c]["all"]
        ]
        one = jnp.where(me == blocks - 1, x3, l1)
        three = jnp.where(me == 0, x3, r1)
        return own + g2 + one + three

    near_gates = gate_sums(0).reshape(local, near_rows)

    near_size = pair * group_size
    token_terms = 0.0
    gate_terms = []
    for e in range(local):
        near_slot = jnp.where(near_rank[e] >= near_rows, -1, near_rank[e])
        near_slot = jnp.concatenate(
            [near_slot, jnp.full(((count - pair) * group_size,), -1, jnp.int32)]
        )
        slot = jnp.where(
            near_slot >= 0, near_slot, jnp.where(all_slot[e] >= 0, all_slot[e] + near_rows, -1)
        )
        chosen = pick(slot, near_rows + far_rows)
        token_terms = token_terms + lax.dot_general(
            chosen.astype(BF16), row_terms[e], (((0,), (0,)), ((), ())),
            preferred_element_type=F32,
        )
        gates = jnp.concatenate([near_gates[e], gate_sums(e + 1)])
        gate_terms.append(jnp.sum(jnp.where(chosen, gates[:, None], 0.0), axis=0))

    gate_table = jnp.stack(gate_terms, axis=1).reshape(count, group_size, local)
    gate_table = gate_table.transpose(0, 2, 1).reshape(count, local * group_size)
    table_rows = -(-EXPERTS * group_size // width)
    table_pad = -(-table_rows // 16) * 16
    placed = lax.dynamic_update_slice(
        jnp.zeros((count, table_pad * width), BF16),
        gate_table.astype(BF16),
        (jnp.int32(0), group * local * group_size),
    ).reshape(count, table_pad, width)
    terms = token_terms.astype(BF16).reshape(count, group_size, width)
    terms = jnp.concatenate([terms, placed], axis=1)

    def plus(a, b):
        return (a.astype(F32) + b.astype(F32)).astype(BF16)

    by_chip = terms.reshape(count // 2, 2, group_size + table_pad, width)
    held = plus(by_chip[:, 0], swap(by_chip[:, 1], 0, count))

    def settle(part, order):
        have = even
        for at, bit in enumerate(order):
            keep = [i for i, o in enumerate(have) if not o >> bit & 1]
            send = [i for i, o in enumerate(have) if o >> bit & 1]
            partner = [have.index(have[i] | (1 << bit)) for i in keep]
            got = swap(jnp.stack([part[i] for i in partner]), bit, count)
            kept = jnp.stack([part[i] for i in keep])
            last = at == len(order) - 1
            part = kept.astype(F32) + got.astype(F32)
            part = part if last else part.astype(BF16)
            have = [have[i] for i in keep]
        return part[0]

    half = width // 2
    settled = jnp.concatenate(
        [settle(held[..., :half], ahead), settle(held[..., half:], ahead[::-1])], axis=1
    )
    grad_tokens = settled[:group_size].astype(BF16)
    table = settled[group_size:].reshape(-1)[: EXPERTS * group_size]
    table = table.reshape(EXPERTS, group_size).T
    named = expert_ids[:, :, None] == jnp.arange(EXPERTS, dtype=jnp.int32)
    grad_gates = jnp.sum(jnp.where(named, table[:, None, :], 0.0), axis=2)
    return (grad_tokens, grad_gates, *grads)


def solution(mesh):
    placed = (
        P("expert", "dp"),
        P("expert", "dp"),
        P("expert", None),
        P("expert", None),
        P("expert", "dp", None),
        P("expert", "dp", None),
        P("expert", None, "dp"),
    )
    return jax.shard_map(
        shards,
        mesh=mesh,
        in_specs=placed,
        out_specs=(
            P("expert", "dp"),
            P("expert", None),
            P("expert", "dp", None),
            P("expert", "dp", None),
            P("expert", None, "dp"),
        ),
        check_vma=False,
    )
```

time: 561 us -> 440 us (0.78)
  waiting for transfers between devices: 306 us -> 51 us
  Pallas kernels: 0 us -> 139 us
  starting transfers between devices: 17.7 us -> 156 us
  blocking collectives: 87.4 us -> 0 us
  matrix products: 79.4 us -> 31.1 us
  local copies, waits for them, and re-layouts: 24.4 us -> 44.2 us
  between operations: 14.6 us -> 1.92 us
  other arithmetic: 22.6 us -> 12.8 us
    reduce_scatter x3 -> x0, waiting for transfers between devices: 221 us -> none  [the longest x1 97.2 us: shards(): lax.psum_scatter(gate_part, 'dp', scatter_dimension=3, tiled=True)]
    ppermute x0 -> x63, starting transfers between devices: none -> 156 us  [the longest x50 142 us: move(): return lax.ppermute(a, 'dp', pairs)]
    pallas_call x0 -> x34, Pallas kernels: none -> 139 us  [the longest x4 47 us: expert_grads(): pl.pallas_call(functools.partial(expert_body, place, near_rows, far_rows,...]
    all_gather x3 -> x0, waiting for transfers between devices: 80.8 us -> none  [the longest x1 45.6 us: shards(): lax.all_gather(grad_up_pre, 'dp', axis=3, tiled=True)]
    all_to_all x3 -> x0, blocking collectives: 73.6 us -> none  [the longest x1 34.6 us: shards(): lax.all_to_all(dy_send, 'expert', split_axis=0, concat_axis=0, tiled=True)]
    ppermute x0 -> x63, waiting for transfers between devices: none -> 51 us  [the longest x50 35.8 us: move(): return lax.ppermute(a, 'dp', pairs)]
    dot_general x10 -> x16, matrix products: 79.4 us -> 31.1 us  [the longest x4 16.2 us: shards(): lax.dot_general(chosen.astype(BF16), row_terms[e], (((0,), (0,)), ((), ()...]
    unnamed x26 -> x122, local copies, waits for them, and re-layouts: 4.48 us -> 29.7 us
  transfers between devices with their start and end apart: 8 -> 63, of which waited for: 7 -> 18; matrix products, arithmetic and copies ran while one was open for 16% -> 12% of each run, Pallas kernels for 0% -> 27%
where the time goes in v1:
time: 440 us; the launch traced here: 436 us
  starting transfers between devices  156 us (35%)
  Pallas kernels  139 us (32%)
  waiting for transfers between devices  51 us (12%)
  local copies, waits for them, and re-layouts  44.2 us (10%)
  matrix products  31.1 us (7%)
  other arithmetic  12.8 us (3%)
    ppermute x50, starting transfers between devices, move(): return lax.ppermute(a, 'dp', pairs)  142 us
    pallas_call x4, Pallas kernels, expert_grads(): pl.pallas_call(functools.partial(expert_body, place, near_rows, far_rows,...  47 us
    pallas_call x5, Pallas kernels, forward(): pl.pallas_call(functools.partial(forward_body, blocks), out_shape=(jax.Sh...  41.8 us
    ppermute x50, waiting for transfers between devices, move(): return lax.ppermute(a, 'dp', pairs)  35.8 us
    unnamed x122, local copies, waits for them, and re-layouts  29.7 us
    pallas_call x10, Pallas kernels, add_blocks(): pl.pallas_call(functools.partial(add_body, pairs), out_shape=[jax.ShapeDt...  29.1 us
    dot_general x4, matrix products, shards(): lax.dot_general(chosen.astype(BF16), row_terms[e], (((0,), (0,)), ((), ()...  16.2 us
    ppermute x13, waiting for transfers between devices, swap(): lax.ppermute(array, 'expert', [(i, i ^ 1 << bit) for i in range(count)])  15.2 us
  transfers between devices with their start and end apart: 63, of which 18 were waited for; matrix products, arithmetic and copies ran while one was open for 12% of the time, Pallas kernels for 27%

profile of v1, /device:TPU:0, one launch (start us, length us, event | category | flops | bytes accessed | tf_op | source)
XLA Modules:
  0.0 436.0 jit_solution(14411088560847436938)
XLA Ops:
  19.6 17.5 %forward_products.5 = (bf16[4,3,256,256]{3,2,1,0:T(8,128)(2,1)}, bf16[3,256,256]{2,1,0:T(8,128)(2,1)}) custom-call(s32[1]{0:T(128)} %bitcast.10.me_ref, bf16[256,1024]{1,0:T(8,128)(2,1)} %convolution_convert_fusion.x_ref.refs_10_, bf16[256,1024]{1,0:T(8,128)(2,1)} %get-tuple-element.108.dy_ref, bf16[4,1024,1024]{2,1,0:T(8,128)(2,1)} %refs_14_.7, ...), custom_call_target="tpu_custom_call" | custom-call | flops 1610612736 | bytes 25165824 | tf_op jit(solution)/shard_map/forward_products/pallas_call | solution.py:46
  37.1 4.5 %collective-permute-start.5 = (bf16[3,256,256]{2,1,0:T(8,128)(2,1)}, bf16[3,256,256]{2,1,0:T(8,128)(2,1)}, u32[]{:S(2)}, u32[]{:S(2)}) collective-permute-start(bf16[3,256,256]{2,1,0:T(8,128)(2,1)} %get-tuple-element.52.refs_2_), channel_id=1, source_target_pairs={{0,1},{3,2},{4,5},{7,6},{8,9},{11,10},{12,13},{15,14},{16,17},{19,... | collective-permute-start | bytes 1179656 | tf_op jit(solution)/shard_map/ppermute | solution.py:431
  51.8 5.0 %collective-permute-start.6 = (bf16[3,256,256]{2,1,0:T(8,128)(2,1)}, bf16[3,256,256]{2,1,0:T(8,128)(2,1)S(1)}, u32[]{:S(2)}, u32[]{:S(2)}) collective-permute-start(bf16[3,256,256]{2,1,0:T(8,128)(2,1)} %hop_sum.10.refs_4_), channel_id=1, source_target_pairs={{0,1},{1,2},{4,5},{5,6},{8,9},{9,10},{12,13},{13,14},{16,17},{17,1... | collective-permute-start | bytes 1179656 | tf_op jit(solution)/shard_map/ppermute | solution.py:431
  56.9 6.5 %collective-permute-done.6.refs_1_ = bf16[3,256,256]{2,1,0:T(8,128)(2,1)S(1)} collective-permute-done((bf16[3,256,256]{2,1,0:T(8,128)(2,1)}, bf16[3,256,256]{2,1,0:T(8,128)(2,1)S(1)}, u32[]{:S(2)}, u32[]{:S(2)}) %collective-permute-start.6) | collective-permute-done | bytes 393248 | tf_op jit(solution)/shard_map/ppermute | solution.py:431
  68.6 5.7 %collective-permute-start.8 = (bf16[3,256,256]{2,1,0:T(8,128)(2,1)}, bf16[3,256,256]{2,1,0:T(8,128)(2,1)}, u32[]{:S(2)}, u32[]{:S(2)}) collective-permute-start(bf16[3,256,256]{2,1,0:T(8,128)(2,1)} %get-tuple-element.53.rest_0_), channel_id=1, source_target_pairs={{0,1},{1,2},{2,3},{4,5},{5,6},{6,7},{8,9},{9,10},{10,11},{12,13},{... | collective-permute-start | bytes 1179656 | tf_op jit(solution)/shard_map/ppermute | solution.py:431
  81.6 6.0 %forward_products.6 = (bf16[4,3,224,256]{3,2,1,0:T(8,128)(2,1)}, bf16[3,224,256]{2,1,0:T(8,128)(2,1)}) custom-call(s32[1]{0:T(128)} %bitcast.10.me_ref, bf16[224,1024]{1,0:T(8,128)(2,1)} %convolution_convert_fusion.4.x_ref.refs_12_, bf16[224,1024]{1,0:T(8,128)(2,1)} %get-tuple-element.116.dy_ref, bf16[4,1024,1024]{2,1,0:T(8,128)(2,1)} %refs_14_.7, ...), custom_call_target="tpu_custom_call" | custom-call | flops 1409286144 | bytes 6291456 | tf_op jit(solution)/shard_map/forward_products/pallas_call | solution.py:46
  87.6 3.5 collective-permute-start.15
  95.5 4.6 %collective-permute-start.13 = (bf16[784,256]{1,0:T(8,128)(2,1)}, bf16[784,256]{1,0:T(8,128)(2,1)S(1)}, u32[]{:S(2)}, u32[]{:S(2)}) collective-permute-start(bf16[784,256]{1,0:T(8,128)(2,1)} %hidden_units.5.refs_2_.refs_0_), channel_id=1, source_target_pairs={{0,1},{1,2},{2,3},{4,5},{5,6},{6,7},{8,9},{9,10},{10,11},{12,13},{... | collective-permute-start | bytes 1204232 | tf_op jit(solution)/shard_map/ppermute | solution.py:431
  129.3 9.2 %collective-permute-start.21 = (bf16[3,224,256]{2,1,0:T(8,128)(2,1)}, bf16[3,224,256]{2,1,0:T(8,128)(2,1)S(1)}, u32[]{:S(2)}, u32[]{:S(2)}) collective-permute-start(bf16[3,224,256]{2,1,0:T(8,128)(2,1)} %get-tuple-element.59.rest_0_), channel_id=1, source_target_pairs={{0,1},{1,2},{2,3},{4,5},{5,6},{6,7},{8,9},{9,10},{10,11},{12,13},{... | collective-permute-start | bytes 1032200 | tf_op jit(solution)/shard_map/ppermute | solution.py:431
  138.5 6.1 %forward_products.7 = (bf16[4,3,224,256]{3,2,1,0:T(8,128)(2,1)}, bf16[3,224,256]{2,1,0:T(8,128)(2,1)}) custom-call(s32[1]{0:T(128)} %bitcast.10.me_ref, bf16[224,1024]{1,0:T(8,128)(2,1)} %convolution_convert_fusion.3.x_ref.refs_12_, bf16[224,1024]{1,0:T(8,128)(2,1)} %get-tuple-element.114.dy_ref, bf16[4,1024,1024]{2,1,0:T(8,128)(2,1)} %refs_14_.7, ...), custom_call_target="tpu_custom_call" | custom-call | flops 1409286144 | bytes 6291456 | tf_op jit(solution)/shard_map/forward_products/pallas_call | solution.py:46
  144.5 3.9 collective-permute-start.25
  162.5 5.2 %collective-permute-start.28 = (bf16[3,224,256]{2,1,0:T(8,128)(2,1)}, bf16[3,224,256]{2,1,0:T(8,128)(2,1)S(1)}, u32[]{:S(2)}, u32[]{:S(2)}) collective-permute-start(bf16[3,224,256]{2,1,0:T(8,128)(2,1)} %hop_sum.14.refs_2_), channel_id=1, source_target_pairs={{0,1},{1,2},{4,5},{5,6},{8,9},{9,10},{12,13},{13,14},{16,17},{17,1... | collective-permute-start | bytes 1032200 | tf_op jit(solution)/shard_map/ppermute | solution.py:431
  169.1 5.2 %collective-permute-start.23 = (bf16[688,256]{1,0:T(8,128)(2,1)S(1)}, bf16[688,256]{1,0:T(8,128)(2,1)S(1)}, u32[]{:S(2)}, u32[]{:S(2)}) collective-permute-start(bf16[688,256]{1,0:T(8,128)(2,1)S(1)} %copy-done.5), channel_id=1, source_target_pairs={{0,1},{1,2},{2,3},{4,5},{5,6},{6,7},{8,9},{9,10},{10,11},{12,13},{... | collective-permute-start | bytes 1056776 | tf_op jit(solution)/shard_map/ppermute | solution.py:431
  186.5 9.9 %collective-permute-start.32 = (bf16[3,224,256]{2,1,0:T(8,128)(2,1)}, bf16[3,224,256]{2,1,0:T(8,128)(2,1)S(1)}, u32[]{:S(2)}, u32[]{:S(2)}) collective-permute-start(bf16[3,224,256]{2,1,0:T(8,128)(2,1)} %get-tuple-element.65.rest_0_), channel_id=1, source_target_pairs={{0,1},{1,2},{2,3},{4,5},{5,6},{6,7},{8,9},{9,10},{10,11},{12,13},{... | collective-permute-start | bytes 1032200 | tf_op jit(solution)/shard_map/ppermute | solution.py:431
  197.6 6.1 %forward_products.8 = (bf16[4,3,224,256]{3,2,1,0:T(8,128)(2,1)}, bf16[3,224,256]{2,1,0:T(8,128)(2,1)}) custom-call(s32[1]{0:T(128)} %bitcast.10.me_ref, bf16[224,1024]{1,0:T(8,128)(2,1)} %convolution_convert_fusion.2.x_ref.refs_12_, bf16[224,1024]{1,0:T(8,128)(2,1)} %get-tuple-element.112.dy_ref, bf16[4,1024,1024]{2,1,0:T(8,128)(2,1)} %refs_14_.7, ...), custom_call_target="tpu_custom_call" | custom-call | flops 1409286144 | bytes 6291456 | tf_op jit(solution)/shard_map/forward_products/pallas_call | solution.py:46
  203.8 4.6 %collective-permute-start.31 = (bf16[3,224,256]{2,1,0:T(8,128)(2,1)}, bf16[3,224,256]{2,1,0:T(8,128)(2,1)S(1)}, u32[]{:S(2)}, u32[]{:S(2)}) collective-permute-start(bf16[3,224,256]{2,1,0:T(8,128)(2,1)} %get-tuple-element.66.rest_0_), channel_id=1, source_target_pairs={{0,1},{3,2},{4,5},{7,6},{8,9},{11,10},{12,13},{15,14},{16,17},{19,... | collective-permute-start | bytes 1032200 | tf_op jit(solution)/shard_map/ppermute | solution.py:431
  223.7 7.1 %collective-permute-start.36 = (bf16[688,256]{1,0:T(8,128)(2,1)S(1)}, bf16[688,256]{1,0:T(8,128)(2,1)S(1)}, u32[]{:S(2)}, u32[]{:S(2)}) collective-permute-start(bf16[688,256]{1,0:T(8,128)(2,1)S(1)} %copy-done.4), channel_id=1, source_target_pairs={{0,1},{1,2},{2,3},{4,5},{5,6},{6,7},{8,9},{9,10},{10,11},{12,13},{... | collective-permute-start | bytes 1056776 | tf_op jit(solution)/shard_map/ppermute | solution.py:431
  243.0 10.1 %collective-permute-start.42 = (bf16[3,224,256]{2,1,0:T(8,128)(2,1)}, bf16[3,224,256]{2,1,0:T(8,128)(2,1)S(1)}, u32[]{:S(2)}, u32[]{:S(2)}) collective-permute-start(bf16[3,224,256]{2,1,0:T(8,128)(2,1)} %get-tuple-element.70.rest_0_), channel_id=1, source_target_pairs={{0,1},{1,2},{2,3},{4,5},{5,6},{6,7},{8,9},{9,10},{10,11},{12,13},{... | collective-permute-start | bytes 1032200 | tf_op jit(solution)/shard_map/ppermute | solution.py:431
  254.4 6.1 %forward_products.9 = (bf16[4,3,224,256]{3,2,1,0:T(8,128)(2,1)}, bf16[3,224,256]{2,1,0:T(8,128)(2,1)}) custom-call(s32[1]{0:T(128)} %bitcast.10.me_ref, bf16[224,1024]{1,0:T(8,128)(2,1)} %convolution_convert_fusion.1.x_ref.refs_12_, bf16[224,1024]{1,0:T(8,128)(2,1)} %get-tuple-element.110.dy_ref, bf16[4,1024,1024]{2,1,0:T(8,128)(2,1)} %refs_14_.7, ...), custom_call_target="tpu_custom_call" | custom-call | flops 1409286144 | bytes 6291456 | tf_op jit(solution)/shard_map/forward_products/pallas_call | solution.py:46
  261.3 4.5 %collective-permute-start.41 = (bf16[3,224,256]{2,1,0:T(8,128)(2,1)}, bf16[3,224,256]{2,1,0:T(8,128)(2,1)S(1)}, u32[]{:S(2)}, u32[]{:S(2)}) collective-permute-start(bf16[3,224,256]{2,1,0:T(8,128)(2,1)} %get-tuple-element.71.refs_16_), channel_id=1, source_target_pairs={{0,1},{3,2},{4,5},{7,6},{8,9},{11,10},{12,13},{15,14},{16,17},{19,... | collective-permute-start | bytes 1032200 | tf_op jit(solution)/shard_map/ppermute | solution.py:431
  265.9 11.7 %expert_grads.4 = (f32[4,1024,1024]{2,1,0:T(8,128)}, f32[4,1024,1024]{2,1,0:T(8,128)}, f32[4,1024,1024]{2,1,0:T(8,128)}, bf16[288,1024]{1,0:T(8,128)(2,1)}) custom-call(s32[1]{0:T(128)} %bitcast.10.me_ref, bf16[784,256]{1,0:T(8,128)(2,1)} %hidden_units.5.refs_2_.refs_0_, bf16[784,256]{1,0:T(8,128)(2,1)} %get-tuple-element.57.refs_1_, ...), custom_call_target="tpu_custom_call" | custom-call | flops 3019898880 | bytes 16777216 | tf_op jit(solution)/shard_map/expert_grads/pallas_call | solution.py:274
  294.7 5.2 %collective-permute-start.46 = (bf16[688,256]{1,0:T(8,128)(2,1)S(1)}, bf16[688,256]{1,0:T(8,128)(2,1)S(1)}, u32[]{:S(2)}, u32[]{:S(2)}) collective-permute-start(bf16[688,256]{1,0:T(8,128)(2,1)S(1)} %copy-done.6), channel_id=1, source_target_pairs={{0,1},{1,2},{2,3},{4,5},{5,6},{6,7},{8,9},{9,10},{10,11},{12,13},{... | collective-permute-start | bytes 1056776 | tf_op jit(solution)/shard_map/ppermute | solution.py:431
  313.0 8.7 %collective-permute-start.51 = (bf16[3,224,256]{2,1,0:T(8,128)(2,1)}, bf16[3,224,256]{2,1,0:T(8,128)(2,1)S(1)}, u32[]{:S(2)}, u32[]{:S(2)}) collective-permute-start(bf16[3,224,256]{2,1,0:T(8,128)(2,1)} %get-tuple-element.80.refs_19_), channel_id=1, source_target_pairs={{0,1},{1,2},{2,3},{4,5},{5,6},{6,7},{8,9},{9,10},{10,11},{12,13},{... | collective-permute-start | bytes 1032200 | tf_op jit(solution)/shard_map/ppermute | solution.py:431
  324.8 11.7 %expert_grads.5 = (f32[4,1024,1024]{2,1,0:T(8,128)}, f32[4,1024,1024]{2,1,0:T(8,128)}, f32[4,1024,1024]{2,1,0:T(8,128)}, bf16[288,1024]{1,0:T(8,128)(2,1)}) custom-call(s32[1]{0:T(128)} %bitcast.10.me_ref, bf16[784,256]{1,0:T(8,128)(2,1)} %hidden_units.5.refs_2_.refs_0_, ...), custom_call_target="tpu_custom_call", output_to_operand_aliasing={{0}: (17, {}), {1}: (18, {}), {2}: (19, {})} | custom-call | flops 3019898880 | bytes 16777216 | tf_op jit(solution)/shard_map/expert_grads/pallas_call | solution.py:274
  336.7 4.4 %fusion.6 = f32[1024,1024]{1,0:T(8,128)} fusion(bf16[288,1024]{1,0:T(8,128)(2,1)} %get-tuple-element.81.rest_0_, s32[1024]{0:T(1024)S(1)} %compare_select_fusion.4), kind=kOutput, calls=%fused_computation.27 | convolution fusion | flops 604274688 | bytes 4788224 | tf_op jit(solution)/shard_map/dot_general | solution.py:513
  349.6 5.2 %collective-permute-start.53 = (bf16[688,256]{1,0:T(8,128)(2,1)}, bf16[688,256]{1,0:T(8,128)(2,1)S(1)}, u32[]{:S(2)}, u32[]{:S(2)}) collective-permute-start(bf16[688,256]{1,0:T(8,128)(2,1)} %hidden_units.9.refs_2_.refs_5_), channel_id=1, source_target_pairs={{0,1},{1,2},{2,3},{4,5},{5,6},{6,7},{8,9},{9,10},{10,11},{12,13},{... | collective-permute-start | bytes 1056776 | tf_op jit(solution)/shard_map/ppermute | solution.py:431
  364.8 11.7 %expert_grads.6 = (f32[4,1024,1024]{2,1,0:T(8,128)}, f32[4,1024,1024]{2,1,0:T(8,128)}, f32[4,1024,1024]{2,1,0:T(8,128)}, bf16[288,1024]{1,0:T(8,128)(2,1)}) custom-call(s32[1]{0:T(128)} %bitcast.10.me_ref, bf16[784,256]{1,0:T(8,128)(2,1)} %hidden_units.5.refs_2_.refs_0_, ...), custom_call_target="tpu_custom_call", output_to_operand_aliasing={{0}: (17, {}), {1}: (18, {}), {2}: (19, {})} | custom-call | flops 3019898880 | bytes 16777216 | tf_op jit(solution)/shard_map/expert_grads/pallas_call | solution.py:274
  377.3 4.4 %fusion.5 = f32[1024,1024]{1,0:T(8,128)} fusion(bf16[288,1024]{1,0:T(8,128)(2,1)} %get-tuple-element.88.rest_0_, s32[1024]{0:T(1024)S(1)} %compare_select_fusion.3), kind=kOutput, calls=%fused_computation.25 | convolution fusion | flops 604274688 | bytes 4788224 | tf_op jit(solution)/shard_map/dot_general | solution.py:513
  387.9 9.5 %collective-permute-done.57.refs_9_ = bf16[688,256]{1,0:T(8,128)(2,1)S(1)} collective-permute-done((bf16[688,256]{1,0:T(8,128)(2,1)}, bf16[688,256]{1,0:T(8,128)(2,1)S(1)}, u32[]{:S(2)}, u32[]{:S(2)}) %collective-permute-start.57) | collective-permute-done | bytes 352288 | tf_op jit(solution)/shard_map/ppermute | solution.py:431
  398.2 11.8 %expert_grads.7 = (f32[4,1024,1024]{2,1,0:T(8,128)}, f32[4,1024,1024]{2,1,0:T(8,128)}, f32[4,1024,1024]{2,1,0:T(8,128)}, bf16[288,1024]{1,0:T(8,128)(2,1)}) custom-call(s32[1]{0:T(128)} %bitcast.10.me_ref, bf16[784,256]{1,0:T(8,128)(2,1)} %hidden_units.5.refs_2_.refs_0_, ...), custom_call_target="tpu_custom_call", output_to_operand_aliasing={{0}: (17, {}), {1}: (18, {}), {2}: (19, {})} | custom-call | flops 3019898880 | bytes 16777216 | tf_op jit(solution)/shard_map/expert_grads/pallas_call | solution.py:274
  410.0 5.1 %add_convert_fusion = bf16[1024,1024]{1,0:T(8,128)(2,1)S(1)} fusion(f32[1024,1024]{1,0:T(8,128)} %fusion.5, f32[1024,1024]{1,0:T(8,128)S(1)} %fusion.7, f32[1024,1024]{1,0:T(8,128)} %fusion.6, bf16[288,1024]{1,0:T(8,128)(2,1)} %get-tuple-element.93, s32[1024]{0:T(1024)S(1)} %compare_select_fusion.2), kind=kOutput, calls=%fused_computation | convolution fusion | flops 608468992 | bytes 15273984 | tf_op jit(solution)/shard_map/dot_general | solution.py:513
  421.9 5.9 %collective-permute-done.61 = bf16[2,144,512]{2,1,0:T(8,128)(2,1)S(1)} collective-permute-done((bf16[2,144,512]{2,1,0:T(8,128)(2,1)S(1)}, bf16[2,144,512]{2,1,0:T(8,128)(2,1)S(1)}, u32[]{:S(2)}, u32[]{:S(2)}) %collective-permute-start.61) | collective-permute-done | bytes 294944 | tf_op jit(solution)/shard_map/ppermute | solution.py:304
  (380 shorter events, 207.5 us)
Async XLA Ops:
  11.9 29.7 %collective-permute-start.11 = (bf16[2,128,1024]{2,1,0:T(8,128)(2,1)S(1)}, bf16[2,128,1024]{2,1,0:T(8,128)(2,1)}, u32[]{:S(2)}, u32[]{:S(2)}) collective-permute-start(bf16[2,128,1024]{2,1,0:T(8,128)(2,1)S(1)} %get-tuple-element.122), channel_id=1, source_target_pairs={{0,8},{4,12},{8,0},{12,4},{16,24},{20,28},{24,16},{28,20},{1,9},{5... | collective-permute-start | bytes 1572872 | tf_op jit(solution)/shard_map/ppermute | solution.py:304
  18.0 25.7 %collective-permute-start.2 = (bf16[2,144,1024]{2,1,0:T(8,128)(2,1)S(1)}, bf16[2,144,1024]{2,1,0:T(8,128)(2,1)S(1)}, u32[]{:S(2)}, u32[]{:S(2)}) collective-permute-start(bf16[2,144,1024]{2,1,0:T(8,128)(2,1)S(1)} %pad_maximum_fusion.6), channel_id=1, source_target_pairs={{0,16},{4,20},{8,24},{12,28},{16,0},{20,4},{24,8},{28,12},{1,17},{... | collective-permute-start | bytes 1769480 | tf_op jit(solution)/shard_map/ppermute | solution.py:304
  43.7 30.6 %collective-permute-start.12 = (bf16[3,128,1024]{2,1,0:T(8,128)(2,1)}, bf16[3,128,1024]{2,1,0:T(8,128)(2,1)S(1)}, u32[]{:S(2)}, u32[]{:S(2)}) collective-permute-start(bf16[3,128,1024]{2,1,0:T(8,128)(2,1)} %get-tuple-element.118), channel_id=1, source_target_pairs={{0,4},{4,0},{8,12},{12,8},{16,20},{20,16},{24,28},{28,24},{1,5},{5... | collective-permute-start | bytes 2359304 | tf_op jit(solution)/shard_map/ppermute | solution.py:304
  43.7 31.8 %collective-permute-start.3 = (bf16[3,144,1024]{2,1,0:T(8,128)(2,1)S(1)}, bf16[3,144,1024]{2,1,0:T(8,128)(2,1)}, u32[]{:S(2)}, u32[]{:S(2)}) collective-permute-start(bf16[3,144,1024]{2,1,0:T(8,128)(2,1)S(1)} %constant_dynamic-update-slice_fusion), channel_id=1, source_target_pairs={{0,4},{4,0},{8,12},{12,8},{16,20},{20,16},{24,28},{28,24},{1,5},{5... | collective-permute-start | bytes 2654216 | tf_op jit(solution)/shard_map/ppermute | solution.py:304
  67.3 23.8 %collective-permute-start.9 = (bf16[3,256,256]{2,1,0:T(8,128)(2,1)}, bf16[3,256,256]{2,1,0:T(8,128)(2,1)}, u32[]{:S(2)}, u32[]{:S(2)}) collective-permute-start(bf16[3,256,256]{2,1,0:T(8,128)(2,1)} %get-tuple-element.54), channel_id=1, source_target_pairs={{1,0},{2,1},{3,2},{5,4},{6,5},{7,6},{9,8},{10,9},{11,10},{13,12},{... | collective-permute-start | bytes 1179656 | tf_op jit(solution)/shard_map/ppermute | solution.py:431
  68.6 22.6 %collective-permute-start.8 = (bf16[3,256,256]{2,1,0:T(8,128)(2,1)}, bf16[3,256,256]{2,1,0:T(8,128)(2,1)}, u32[]{:S(2)}, u32[]{:S(2)}) collective-permute-start(bf16[3,256,256]{2,1,0:T(8,128)(2,1)} %get-tuple-element.53.rest_0_), channel_id=1, source_target_pairs={{0,1},{1,2},{2,3},{4,5},{5,6},{6,7},{8,9},{9,10},{10,11},{12,13},{... | collective-permute-start | bytes 1179656 | tf_op jit(solution)/shard_map/ppermute | solution.py:431
  87.6 22.3 %collective-permute-start.15 = (bf16[3,224,256]{2,1,0:T(8,128)(2,1)}, bf16[3,224,256]{2,1,0:T(8,128)(2,1)S(1)}, u32[]{:S(2)}, u32[]{:S(2)}) collective-permute-start(bf16[3,224,256]{2,1,0:T(8,128)(2,1)} %get-tuple-element.55.rest_0_), channel_id=1, source_target_pairs={{0,1},{3,2},{4,5},{7,6},{8,9},{11,10},{12,13},{15,14},{16,17},{19,... | collective-permute-start | bytes 1032200 | tf_op jit(solution)/shard_map/ppermute | solution.py:431
  94.3 22.4 %collective-permute-start.14 = (bf16[784,256]{1,0:T(8,128)(2,1)}, bf16[784,256]{1,0:T(8,128)(2,1)S(1)}, u32[]{:S(2)}, u32[]{:S(2)}) collective-permute-start(bf16[784,256]{1,0:T(8,128)(2,1)} %hidden_units.5.refs_2_.refs_0_), channel_id=1, source_target_pairs={{1,0},{2,1},{3,2},{5,4},{6,5},{7,6},{9,8},{10,9},{11,10},{13,12},{... | collective-permute-start | bytes 1204232 | tf_op jit(solution)/shard_map/ppermute | solution.py:431
  95.5 21.1 %collective-permute-start.13 = (bf16[784,256]{1,0:T(8,128)(2,1)}, bf16[784,256]{1,0:T(8,128)(2,1)S(1)}, u32[]{:S(2)}, u32[]{:S(2)}) collective-permute-start(bf16[784,256]{1,0:T(8,128)(2,1)} %hidden_units.5.refs_2_.refs_0_), channel_id=1, source_target_pairs={{0,1},{1,2},{2,3},{4,5},{5,6},{6,7},{8,9},{9,10},{10,11},{12,13},{... | collective-permute-start | bytes 1204232 | tf_op jit(solution)/shard_map/ppermute | solution.py:431
  118.2 31.0 %collective-permute-start.17 = (bf16[784,256]{1,0:T(8,128)(2,1)}, bf16[784,256]{1,0:T(8,128)(2,1)S(1)}, u32[]{:S(2)}, u32[]{:S(2)}) collective-permute-start(bf16[784,256]{1,0:T(8,128)(2,1)} %get-tuple-element.57.refs_1_), channel_id=1, source_target_pairs={{2,1},{1,0},{6,5},{5,4},{10,9},{9,8},{14,13},{13,12},{18,17},{17,1... | collective-permute-start | bytes 1204232 | tf_op jit(solution)/shard_map/ppermute | solution.py:431
  119.5 29.7 %collective-permute-start.16 = (bf16[784,256]{1,0:T(8,128)(2,1)}, bf16[784,256]{1,0:T(8,128)(2,1)S(1)}, u32[]{:S(2)}, u32[]{:S(2)}) collective-permute-start(bf16[784,256]{1,0:T(8,128)(2,1)} %get-tuple-element.58.refs_4_.refs_2_), channel_id=1, source_target_pairs={{1,2},{2,3},{5,6},{6,7},{9,10},{10,11},{13,14},{14,15},{17,18},{18... | collective-permute-start | bytes 1204232 | tf_op jit(solution)/shard_map/ppermute | solution.py:431
  128.0 26.7 %collective-permute-start.22 = (bf16[3,224,256]{2,1,0:T(8,128)(2,1)}, bf16[3,224,256]{2,1,0:T(8,128)(2,1)S(1)}, u32[]{:S(2)}, u32[]{:S(2)}) collective-permute-start(bf16[3,224,256]{2,1,0:T(8,128)(2,1)} %get-tuple-element.61), channel_id=1, source_target_pairs={{1,0},{2,1},{3,2},{5,4},{6,5},{7,6},{9,8},{10,9},{11,10},{13,12},{... | collective-permute-start | bytes 1032200 | tf_op jit(solution)/shard_map/ppermute | solution.py:431
  129.3 25.4 %collective-permute-start.21 = (bf16[3,224,256]{2,1,0:T(8,128)(2,1)}, bf16[3,224,256]{2,1,0:T(8,128)(2,1)S(1)}, u32[]{:S(2)}, u32[]{:S(2)}) collective-permute-start(bf16[3,224,256]{2,1,0:T(8,128)(2,1)} %get-tuple-element.59.rest_0_), channel_id=1, source_target_pairs={{0,1},{1,2},{2,3},{4,5},{5,6},{6,7},{8,9},{9,10},{10,11},{12,13},{... | collective-permute-start | bytes 1032200 | tf_op jit(solution)/shard_map/ppermute | solution.py:431
  152.7 21.6 %collective-permute-start.20 = (bf16[784,256]{1,0:T(8,128)(2,1)}, bf16[784,256]{1,0:T(8,128)(2,1)S(1)}, u32[]{:S(2)}, u32[]{:S(2)}) collective-permute-start(bf16[784,256]{1,0:T(8,128)(2,1)} %hop_join.5.rest_0_.refs_3_), channel_id=1, source_target_pairs={{2,3},{1,0},{6,7},{5,4},{10,11},{9,8},{14,15},{13,12},{18,19},{17,... | collective-permute-start | bytes 1204232 | tf_op jit(solution)/shard_map/ppermute | solution.py:431
  161.9 18.8 %collective-permute-start.29 = (bf16[3,224,256]{2,1,0:T(8,128)(2,1)}, bf16[3,224,256]{2,1,0:T(8,128)(2,1)S(1)}, u32[]{:S(2)}, u32[]{:S(2)}) collective-permute-start(bf16[3,224,256]{2,1,0:T(8,128)(2,1)} %hop_sum.14.refs_2_), channel_id=1, source_target_pairs={{3,2},{2,1},{7,6},{6,5},{11,10},{10,9},{15,14},{14,13},{19,18},{18... | collective-permute-start | bytes 1032200 | tf_op jit(solution)/shard_map/ppermute | solution.py:431
  162.5 18.1 %collective-permute-start.28 = (bf16[3,224,256]{2,1,0:T(8,128)(2,1)}, bf16[3,224,256]{2,1,0:T(8,128)(2,1)S(1)}, u32[]{:S(2)}, u32[]{:S(2)}) collective-permute-start(bf16[3,224,256]{2,1,0:T(8,128)(2,1)} %hop_sum.14.refs_2_), channel_id=1, source_target_pairs={{0,1},{1,2},{4,5},{5,6},{8,9},{9,10},{12,13},{13,14},{16,17},{17,1... | collective-permute-start | bytes 1032200 | tf_op jit(solution)/shard_map/ppermute | solution.py:431
  179.8 29.3 %collective-permute-start.26 = (bf16[688,256]{1,0:T(8,128)(2,1)}, bf16[688,256]{1,0:T(8,128)(2,1)S(1)}, u32[]{:S(2)}, u32[]{:S(2)}) collective-permute-start(bf16[688,256]{1,0:T(8,128)(2,1)} %get-tuple-element.64.refs_4_.refs_7_), channel_id=1, source_target_pairs={{1,2},{2,3},{5,6},{6,7},{9,10},{10,11},{13,14},{14,15},{17,18},{18... | collective-permute-start | bytes 1056776 | tf_op jit(solution)/shard_map/ppermute | solution.py:431
  185.2 27.2 %collective-permute-start.33 = (bf16[3,224,256]{2,1,0:T(8,128)(2,1)}, bf16[3,224,256]{2,1,0:T(8,128)(2,1)S(1)}, u32[]{:S(2)}, u32[]{:S(2)}) collective-permute-start(bf16[3,224,256]{2,1,0:T(8,128)(2,1)} %get-tuple-element.68), channel_id=1, source_target_pairs={{1,0},{2,1},{3,2},{5,4},{6,5},{7,6},{9,8},{10,9},{11,10},{13,12},{... | collective-permute-start | bytes 1032200 | tf_op jit(solution)/shard_map/ppermute | solution.py:431
  186.5 26.0 %collective-permute-start.32 = (bf16[3,224,256]{2,1,0:T(8,128)(2,1)}, bf16[3,224,256]{2,1,0:T(8,128)(2,1)S(1)}, u32[]{:S(2)}, u32[]{:S(2)}) collective-permute-start(bf16[3,224,256]{2,1,0:T(8,128)(2,1)} %get-tuple-element.65.rest_0_), channel_id=1, source_target_pairs={{0,1},{1,2},{2,3},{4,5},{5,6},{6,7},{8,9},{9,10},{10,11},{12,13},{... | collective-permute-start | bytes 1032200 | tf_op jit(solution)/shard_map/ppermute | solution.py:431
  230.8 30.4 %collective-permute-start.30 = (bf16[688,256]{1,0:T(8,128)(2,1)S(1)}, bf16[688,256]{1,0:T(8,128)(2,1)S(1)}, u32[]{:S(2)}, u32[]{:S(2)}) collective-permute-start(bf16[688,256]{1,0:T(8,128)(2,1)S(1)} %copy-done.10), channel_id=1, source_target_pairs={{2,3},{1,0},{6,7},{5,4},{10,11},{9,8},{14,15},{13,12},{18,19},{17,... | collective-permute-start | bytes 1056776 | tf_op jit(solution)/shard_map/ppermute | solution.py:431
  236.4 43.9 %collective-permute-start.38 = (bf16[688,256]{1,0:T(8,128)(2,1)}, bf16[688,256]{1,0:T(8,128)(2,1)S(1)}, u32[]{:S(2)}, u32[]{:S(2)}) collective-permute-start(bf16[688,256]{1,0:T(8,128)(2,1)} %get-tuple-element.69.refs_4_.refs_7_), channel_id=1, source_target_pairs={{1,2},{2,3},{5,6},{6,7},{9,10},{10,11},{13,14},{14,15},{17,18},{18... | collective-permute-start | bytes 1056776 | tf_op jit(solution)/shard_map/ppermute | solution.py:431
  241.7 41.9 %collective-permute-start.43 = (bf16[3,224,256]{2,1,0:T(8,128)(2,1)}, bf16[3,224,256]{2,1,0:T(8,128)(2,1)S(1)}, u32[]{:S(2)}, u32[]{:S(2)}) collective-permute-start(bf16[3,224,256]{2,1,0:T(8,128)(2,1)} %get-tuple-element.78), channel_id=1, source_target_pairs={{1,0},{2,1},{3,2},{5,4},{6,5},{7,6},{9,8},{10,9},{11,10},{13,12},{... | collective-permute-start | bytes 1032200 | tf_op jit(solution)/shard_map/ppermute | solution.py:431
  243.0 40.6 %collective-permute-start.42 = (bf16[3,224,256]{2,1,0:T(8,128)(2,1)}, bf16[3,224,256]{2,1,0:T(8,128)(2,1)S(1)}, u32[]{:S(2)}, u32[]{:S(2)}) collective-permute-start(bf16[3,224,256]{2,1,0:T(8,128)(2,1)} %get-tuple-element.70.rest_0_), channel_id=1, source_target_pairs={{0,1},{1,2},{2,3},{4,5},{5,6},{6,7},{8,9},{9,10},{10,11},{12,13},{... | collective-permute-start | bytes 1032200 | tf_op jit(solution)/shard_map/ppermute | solution.py:431
  253.1 27.1 %collective-permute-start.39 = (bf16[688,256]{1,0:T(8,128)(2,1)S(1)}, bf16[688,256]{1,0:T(8,128)(2,1)S(1)}, u32[]{:S(2)}, u32[]{:S(2)}) collective-permute-start(bf16[688,256]{1,0:T(8,128)(2,1)S(1)} %copy-done.17), channel_id=1, source_target_pairs={{2,1},{1,0},{6,5},{5,4},{10,9},{9,8},{14,13},{13,12},{18,17},{17,1... | collective-permute-start | bytes 1056776 | tf_op jit(solution)/shard_map/ppermute | solution.py:431
  261.3 26.1 %collective-permute-start.41 = (bf16[3,224,256]{2,1,0:T(8,128)(2,1)}, bf16[3,224,256]{2,1,0:T(8,128)(2,1)S(1)}, u32[]{:S(2)}, u32[]{:S(2)}) collective-permute-start(bf16[3,224,256]{2,1,0:T(8,128)(2,1)} %get-tuple-element.71.refs_16_), channel_id=1, source_target_pairs={{0,1},{3,2},{4,5},{7,6},{8,9},{11,10},{12,13},{15,14},{16,17},{19,... | collective-permute-start | bytes 1032200 | tf_op jit(solution)/shard_map/ppermute | solution.py:431
  299.9 24.1 %collective-permute-start.40 = (bf16[688,256]{1,0:T(8,128)(2,1)S(1)}, bf16[688,256]{1,0:T(8,128)(2,1)S(1)}, u32[]{:S(2)}, u32[]{:S(2)}) collective-permute-start(bf16[688,256]{1,0:T(8,128)(2,1)S(1)} %copy-done.11), channel_id=1, source_target_pairs={{2,3},{1,0},{6,7},{5,4},{10,11},{9,8},{14,15},{13,12},{18,19},{17,... | collective-permute-start | bytes 1056776 | tf_op jit(solution)/shard_map/ppermute | solution.py:431
  306.4 34.8 %collective-permute-start.48 = (bf16[688,256]{1,0:T(8,128)(2,1)}, bf16[688,256]{1,0:T(8,128)(2,1)S(1)}, u32[]{:S(2)}, u32[]{:S(2)}) collective-permute-start(bf16[688,256]{1,0:T(8,128)(2,1)} %get-tuple-element.79.refs_4_.refs_7_), channel_id=1, source_target_pairs={{1,2},{2,3},{5,6},{6,7},{9,10},{10,11},{13,14},{14,15},{17,18},{18... | collective-permute-start | bytes 1056776 | tf_op jit(solution)/shard_map/ppermute | solution.py:431
  311.8 32.8 %collective-permute-start.52 = (bf16[3,224,256]{2,1,0:T(8,128)(2,1)}, bf16[3,224,256]{2,1,0:T(8,128)(2,1)S(1)}, u32[]{:S(2)}, u32[]{:S(2)}) collective-permute-start(bf16[3,224,256]{2,1,0:T(8,128)(2,1)} %get-tuple-element.86), channel_id=1, source_target_pairs={{1,0},{2,1},{3,2},{5,4},{6,5},{7,6},{9,8},{10,9},{11,10},{13,12},{... | collective-permute-start | bytes 1032200 | tf_op jit(solution)/shard_map/ppermute | solution.py:431
  313.0 31.5 %collective-permute-start.51 = (bf16[3,224,256]{2,1,0:T(8,128)(2,1)}, bf16[3,224,256]{2,1,0:T(8,128)(2,1)S(1)}, u32[]{:S(2)}, u32[]{:S(2)}) collective-permute-start(bf16[3,224,256]{2,1,0:T(8,128)(2,1)} %get-tuple-element.80.refs_19_), channel_id=1, source_target_pairs={{0,1},{1,2},{2,3},{4,5},{5,6},{6,7},{8,9},{9,10},{10,11},{12,13},{... | collective-permute-start | bytes 1032200 | tf_op jit(solution)/shard_map/ppermute | solution.py:431
  321.8 19.3 %collective-permute-start.49 = (bf16[688,256]{1,0:T(8,128)(2,1)S(1)}, bf16[688,256]{1,0:T(8,128)(2,1)S(1)}, u32[]{:S(2)}, u32[]{:S(2)}) collective-permute-start(bf16[688,256]{1,0:T(8,128)(2,1)S(1)} %copy-done.19), channel_id=1, source_target_pairs={{2,1},{1,0},{6,5},{5,4},{10,9},{9,8},{14,13},{13,12},{18,17},{17,1... | collective-permute-start | bytes 1056776 | tf_op jit(solution)/shard_map/ppermute | solution.py:431
  360.7 20.9 %collective-permute-start.56 = (bf16[688,256]{1,0:T(8,128)(2,1)}, bf16[688,256]{1,0:T(8,128)(2,1)S(1)}, u32[]{:S(2)}, u32[]{:S(2)}) collective-permute-start(bf16[688,256]{1,0:T(8,128)(2,1)} %get-tuple-element.89.refs_6_), channel_id=1, source_target_pairs={{2,1},{1,0},{6,5},{5,4},{10,9},{9,8},{14,13},{13,12},{18,17},{17,1... | collective-permute-start | bytes 1056776 | tf_op jit(solution)/shard_map/ppermute | solution.py:431
  362.0 19.7 %collective-permute-start.55 = (bf16[688,256]{1,0:T(8,128)(2,1)}, bf16[688,256]{1,0:T(8,128)(2,1)S(1)}, u32[]{:S(2)}, u32[]{:S(2)}) collective-permute-start(bf16[688,256]{1,0:T(8,128)(2,1)} %get-tuple-element.87.refs_19_.refs_7_), channel_id=1, source_target_pairs={{1,2},{2,3},{5,6},{6,7},{9,10},{10,11},{13,14},{14,15},{17,18},{18... | collective-permute-start | bytes 1056776 | tf_op jit(solution)/shard_map/ppermute | solution.py:431
  (89 other events, 511.7 us)
